TPU v7x, 256 devices: a whole 4x4x8 slice. The times are simulated.
256 devices in a mesh: ctx: 32 (over z, y_hi, core), tp: 8 (over x, y_lo).
Axes of the slice: x: 4, y: 4 (y_hi: 2, y_lo: 2; y = y_hi * 2 + y_lo), z: 8, core: 2. Of those that a mesh axis runs over, the one named last changes fastest.
Arguments:
- query_act: bfloat16 [16384, 4096], P('ctx', 'tp'), may hold values from -6 to 6
- key_act: bfloat16 [16384, 4096], P('ctx', 'tp'), may hold values from -6 to 6
- value_act: bfloat16 [16384, 4096], P('ctx', 'tp'), may hold values from -6 to 6
- filters: float32 [128, 4096], P(None, 'tp'), may hold values from -1.25 to 1.25
- out_weight: bfloat16 [4096, 4096], P('ctx', 'tp'), may hold values from -0.09375 to 0.09375
- grad_out: bfloat16 [16384, 4096], P('ctx', 'tp'), may hold values from -6 to 6
Outputs:
- grad_query: bfloat16 [16384, 4096], P('ctx', 'tp')
- grad_key: bfloat16 [16384, 4096], P('ctx', 'tp')
- grad_value: bfloat16 [16384, 4096], P('ctx', 'tp')
- grad_filters: float32 [128, 4096], P(None, 'tp')
- grad_weight: bfloat16 [4096, 4096], P('ctx', 'tp')
All inputs are finite; a program needn't handle non-finite values.
Results may differ from a plain program's by a relative error of at most 0.0058.
Values may be sent and summed in bfloat16 or wider, within the bound.
A program may use at most 128 MiB of HBM per device.

v0:
```python
import jax
import jax.numpy as jnp
from jax import lax
from jax.sharding import PartitionSpec as P

tap_group = 16


def from_behind(value, axis, by):
    count = lax.axis_size(axis)
    pairs = [(i, i + by) for i in range(count) if 0 <= i + by < count]
    return lax.ppermute(value, axis, pairs)


def tap_sum(source, filters, length, sign, anchor):
    taps = filters.shape[0]

    def tap_step(group, total):
        for offset in range(tap_group):
            tap = group * tap_group + offset
            row = lax.dynamic_slice_in_dim(filters, tap, 1, 0)
            window = lax.dynamic_slice_in_dim(source, anchor + sign * tap, length, 0).astype(
                jnp.float32
            )
            total = total + row * window
        return total

    return lax.fori_loop(
        0, taps // tap_group, tap_step, jnp.zeros((length, source.shape[1]), jnp.float32)
    )


def filter_grad(grad_acc, extended, taps):
    length = grad_acc.shape[0]

    def filter_step(group, result):
        rows = []
        for offset in range(tap_group):
            tap = group * tap_group + offset
            window = lax.dynamic_slice_in_dim(extended, taps - 1 - tap, length, 0).astype(
                jnp.float32
            )
            rows.append(jnp.sum(grad_acc * window, axis=0))
        return lax.dynamic_update_slice_in_dim(result, jnp.stack(rows), group * tap_group, 0)

    return lax.fori_loop(
        0, taps // tap_group, filter_step, jnp.zeros((taps, grad_acc.shape[1]), jnp.float32)
    )


def local(query_act, key_act, value_act, filters, out_weight, grad_out):
    tokens = query_act.shape[0]
    taps = filters.shape[0]
    product = (key_act.astype(jnp.float32) * value_act.astype(jnp.float32)).astype(jnp.bfloat16)
    rim = from_behind(product[tokens - (taps - 1) :], "ctx", 1)
    extended = jnp.concatenate([rim, product], axis=0)
    conv_out = tap_sum(extended, filters, tokens, -1, taps - 1)
    gated = (query_act.astype(jnp.float32) * conv_out).astype(jnp.bfloat16)
    full_grad = lax.all_gather(grad_out, "tp", axis=1, tiled=True)
    grad_gated = jnp.dot(
        full_grad,
        lax.all_gather(out_weight, "ctx", axis=0, tiled=True),
        preferred_element_type=jnp.float32,
    )
    owned = lax.all_to_all(full_grad, "ctx", split_axis=1, concat_axis=0, tiled=True)
    weight_sum = lax.dot_general(
        owned,
        lax.all_gather(gated, "ctx", axis=0, tiled=True),
        (((0,), (0,)), ((), ())),
        preferred_element_type=jnp.float32,
    )
    grad_weight = weight_sum.astype(jnp.bfloat16)
    grad_query = (grad_gated * conv_out).astype(jnp.bfloat16)
    grad_acc = grad_gated * query_act.astype(jnp.float32)
    rim_back = from_behind(grad_acc[: taps - 1], "ctx", -1)
    grad_ext = jnp.concatenate([grad_acc, rim_back], axis=0)
    grad_product = tap_sum(grad_ext, filters, tokens, 1, 0)
    grad_key = (grad_product * value_act.astype(jnp.float32)).astype(jnp.bfloat16)
    grad_value = (grad_product * key_act.astype(jnp.float32)).astype(jnp.bfloat16)
    grad_filters = lax.psum(filter_grad(grad_acc, extended, taps), "ctx")
    return (grad_query, grad_key, grad_value, grad_filters, grad_weight)


def solution(mesh):
    placed = (
        P("ctx", "tp"),
        P("ctx", "tp"),
        P("ctx", "tp"),
        P(None, "tp"),
        P("ctx", "tp"),
        P("ctx", "tp"),
    )
    return jax.shard_map(
        local,
        mesh=mesh,
        in_specs=placed,
        out_specs=(P("ctx", "tp"), P("ctx", "tp"), P("ctx", "tp"), P(None, "tp"), P("ctx", "tp")),
        check_vma=False,
    )
```

profile of v0, /device:TPU:1, one launch (start us, length us, event | category | flops | bytes accessed | tf_op | source)
XLA Modules:
  0.0 669.6 jit_solution(12927477025134899785)
XLA Ops:
  11.5 6.2 collective-permute-start
  19.7 43.1 %while.50 = (s32[]{:T(128)}, f32[512,512]{1,0:T(8,128)S(1)}, f32[128,512]{1,0:T(8,128)}, bf16[639,512]{1,0:T(8,128)(2,1)S(1)}, s32[]{:T(128)}, /*index=5*/s32[]{...) while((s32[]{:T(128)}, f32[512,512]{1,0:T(8,128)S(1)}, ...), condition=%wide.region_1.0_spmd.clone, body=%wide.region_0.0_spmd.clone.sunk | while | flops 12845203 | bytes 10586223 | solution.py:28
  21.1 4.0 fusion.42
  26.6 4.0 fusion.42
  32.0 4.0 fusion.42
  37.3 4.0 fusion.42
  42.7 4.0 fusion.42
  48.1 4.0 fusion.42
  53.5 4.0 fusion.42
  58.8 4.0 fusion.42
  62.9 43.6 %all-gather.4.cloned.1.call-done = bf16[512,4096]{0,1:T(8,128)(2,1)} async-done(((bf16[512,512]{0,1:T(8,128)(2,1)}), bf16[512,4096]{0,1:T(8,128)(2,1)}) %all-gather.4.cloned.1.call-update) | async-done | bytes 4194320 | tf_op jit(solution)/shard_map/all_gather | solution.py:59
  106.5 92.6 %all-gather.6.cloned.1.call-done = bf16[4096,512]{1,0:T(8,128)(2,1)} async-done(((bf16[128,512]{1,0:T(8,128)(2,1)}), bf16[4096,512]{1,0:T(8,128)(2,1)}) %all-gather.6.cloned.1.call-update) | async-done | bytes 4194320 | tf_op jit(solution)/shard_map/all_gather | solution.py:62
  199.1 5.8 fusion.35
  206.2 4.7 all-to-all-start
  213.6 33.5 %while.49 = (s32[]{:T(128)}, f32[128,512]{1,0:T(8,128)S(1)}, bf16[639,512]{1,0:T(8,128)(2,1)S(1)}, f32[512,512]{1,0:T(8,128)S(1)}, s32[]{:T(128)}, /*index=5*/s3...) while((s32[]{:T(128)}, f32[128,512]{1,0:T(8,128)S(1)}, ...), condition=%wide.region_21.0_spmd, body=%wide.region_4.0_spmd.sunk | while | flops 12574805 | bytes 9602267 | solution.py:46
  213.7 4.0 multiply_reduce_fusion.17
  217.8 4.0 multiply_reduce_fusion.17
  226.2 4.0 multiply_reduce_fusion.17
  248.8 35.1 %while.51 = (s32[]{:T(128)}, f32[512,512]{1,0:T(8,128)S(1)}, f32[128,512]{1,0:T(8,128)}, f32[639,512]{1,0:T(8,128)S(1)}, s32[]{:T(128)}, /*index=5*/s32[]{:T(128...) while((s32[]{:T(128)}, f32[512,512]{1,0:T(8,128)S(1)}, ...), condition=%wide.region_3.0_spmd.clone, body=%wide.region_2.0_spmd.clone.sunk | while | flops 8650851 | bytes 18974396 | solution.py:28
  285.2 49.7 %all-to-all-done = bf16[512,32,128]{0,2,1:T(8,128)(2,1)} async-done(((bf16[512,32,128]{0,2,1:T(8,128)(2,1)}), bf16[512,32,128]{0,2,1:T(8,128)(2,1)}, u32[]{:S(2)}, u32[]{:S(2)}) %all-to-all-start) | async-done | bytes 4194336 | tf_op jit(solution)/shard_map/all_to_all | solution.py:65
  334.8 6.4 copy.14
  341.2 53.1 %all-gather.8.cloned.1.call-done = bf16[16384,512]{1,0:T(8,128)(2,1)} async-done(((bf16[512,512]{1,0:T(8,128)(2,1)}), bf16[16384,512]{1,0:T(8,128)(2,1)}) %all-gather.8.cloned.1.call-update) | async-done | bytes 16777232 | tf_op jit(solution)/shard_map/all_gather | solution.py:68
  394.3 11.5 %fusion.30 = bf16[128,512]{0,1:T(8,128)(2,1)S(1)} fusion(bf16[16384,512]{1,0:T(8,128)(2,1)} %all-gather.8.cloned.1.call-done, bf16[16384,128]{1,0:T(8,128)(2,1)} %bitcast.154), kind=kOutput, calls=%fused_computation.88 | convolution fusion | flops 2147549184 | bytes 21102592 | tf_op jit(solution)/shard_map/dot_general | solution.py:66
  406.6 254.9 %all-reduce.2.cloned.1.call-done = f32[128,512]{1,0:T(8,128)} async-done(((f32[128,512]{1,0:T(8,128)}), f32[128,512]{1,0:T(8,128)}) %all-reduce.2.cloned.1.call-update) | async-done | bytes 262160 | tf_op jit(solution)/shard_map/psum | solution.py:80
  (77 shorter events, 79.1 us)
Async XLA Ops:
  7.2 99.3 %all-gather.4.cloned.1.call-start = ((), (), s32[]{:S(2)}) async-start(), calls=%async_computation.1 | async-start | bytes 4718592 | tf_op jit(solution)/shard_map/all_gather | solution.py:59
  9.3 189.8 %all-gather.6.cloned.1.call-start = ((), (), s32[]{:S(2)}) async-start(), calls=%async_computation.2 | async-start | bytes 4325376 | tf_op jit(solution)/shard_map/all_gather | solution.py:62
  10.0 384.3 %all-gather.8.cloned.1.call-start = ((), (), s32[]{:S(2)}) async-start(), calls=%async_computation.4 | async-start | bytes 17301504 | tf_op jit(solution)/shard_map/all_gather | solution.py:68
  11.5 8.1 %collective-permute-start = (bf16[127,512]{1,0:T(8,128)(2,1)S(1)}, bf16[127,512]{1,0:T(8,128)(2,1)S(1)}, u32[]{:S(2)}, u32[]{:S(2)}) collective-permute-start(bf16[127,512]{1,0:T(8,128)(2,1)S(1)} %slice.8), channel_id=1, source_target_pairs={{0,8},{8,16},{16,24},{24,32},{32,40},{40,48},{48,56},{56,64},{64,7... | collective-permute-start | bytes 390152 | tf_op jit(solution)/shard_map/ppermute | solution.py:12
  62.9 142.0 %copy-start.3 = (bf16[512,512]{1,0:T(8,128)(2,1)S(1)}, bf16[512,512]{1,0:T(8,128)(2,1)}, u32[]{:S(2)}) copy-start(bf16[512,512]{1,0:T(8,128)(2,1)} %param.12) | copy-start | bytes 1572868
  206.2 128.6 %all-to-all-start = ((bf16[512,32,128]{0,2,1:T(8,128)(2,1)}), bf16[512,32,128]{0,2,1:T(8,128)(2,1)}, u32[]{:S(2)}, u32[]{:S(2)}) async-start(bf16[512,32,128]{0,2,1:T(8,128)(2,1)} %bitcast.153), calls=%async_computation | async-start | bytes 8388608 | tf_op jit(solution)/shard_map/all_to_all | solution.py:65
  210.9 450.5 %all-reduce.2.cloned.1.call-start = ((), (), s32[]{:S(2)}) async-start(), calls=%async_computation.3 | async-start | bytes 524288 | tf_op jit(solution)/shard_map/psum | solution.py:80
  211.0 36.7 %collective-permute-start.1 = (f32[127,512]{1,0:T(8,128)S(1)}, f32[127,512]{1,0:T(8,128)}, u32[]{:S(2)}, u32[]{:S(2)}) collective-permute-start(f32[127,512]{1,0:T(8,128)S(1)} %slice.9), channel_id=1, source_target_pairs={{8,0},{16,8},{24,16},{32,24},{40,32},{48,40},{56,48},{64,56},{72,6... | collective-permute-start | bytes 780296 | tf_op jit(solution)/shard_map/ppermute | solution.py:12
  247.0 0.7 copy-start.2
  248.8 35.1 %copy-start = (bf16[512,512]{1,0:T(8,128)(2,1)S(1)}, bf16[512,512]{1,0:T(8,128)(2,1)}, u32[]{:S(2)}) copy-start(bf16[512,512]{1,0:T(8,128)(2,1)} %param.14) | copy-start | bytes 1572868
  248.8 35.1 %copy-start.1 = (bf16[512,512]{1,0:T(8,128)(2,1)S(1)}, bf16[512,512]{1,0:T(8,128)(2,1)}, u32[]{:S(2)}) copy-start(bf16[512,512]{1,0:T(8,128)(2,1)} %param.13) | copy-start | bytes 1572868
Sparse Core Ops, SparseCore 0:
  10.4 96.0 all-gather.3
  109.3 89.7 all-gather.5
  206.3 187.9 all-gather.7
  397.3 264.0 all-reduce.1
where the time goes:
time: 671 us; the launch traced here: 670 us
  waiting for transfers between devices  496 us (74%)
  other arithmetic  94 us (14%)
  local copies, waits for them, and re-layouts  30.5 us (5%)
  matrix products  17.3 us (3%)
  between operations  13.9 us (2%)
  starting transfers between devices  13.6 us (2%)
    psum x1, waiting for transfers between devices, local(): grad_filters = lax.psum(filter_grad(grad_acc, extended, taps), 'ctx')  255 us
    all_gather x1, waiting for transfers between devices, local(): lax.all_gather(out_weight, 'ctx', axis=0, tiled=True)  92.6 us
    add x16, other arithmetic, tap_step(): total = total + row * window  57.1 us
    all_gather x1, waiting for transfers between devices, local(): lax.all_gather(gated, 'ctx', axis=0, tiled=True)  53.1 us
    all_to_all x1, waiting for transfers between devices, local(): lax.all_to_all(full_grad, 'ctx', split_axis=1, concat_axis=0, tiled=True)  49.7 us
    all_gather x1, waiting for transfers between devices, local(): full_grad = lax.all_gather(grad_out, 'tp', axis=1, tiled=True)  43.6 us
    reduce_sum x8, other arithmetic, filter_step(): rows.append(jnp.sum(grad_acc * window, axis=0))  31.8 us
    dynamic_slice x16, local copies, waits for them, and re-layouts, tap_step(): row = lax.dynamic_slice_in_dim(filters, tap, 1, 0)  18.1 us
  transfers between devices with their start and end apart: 7, of which 6 were waited for; matrix products, arithmetic and copies ran while one was open for 19% of the time, Pallas kernels for 0%

commit v1 on v0

v1 whole, which is shorter than its diff:
```python
import jax
import jax.numpy as jnp
from jax import lax
from jax.experimental import pallas as pl
from jax.experimental.pallas import tpu as pltpu
from jax.sharding import PartitionSpec as P

MESH = pl.DeviceIdType.MESH
BF16 = jnp.bfloat16
F32 = jnp.float32


def lanes(group):
    return pl.ds(group * 128, 128)


def kernel(
    q_ref, k_ref, v_ref, f_ref, w_hbm, g_hbm,
    gq_ref, gk_ref, gv_ref, gf_ref, gw_ref,
    G, S, W, ext, conv, ga, gg, filt, gt_own, gt_sib,
    halo_s, halo_r, back_s, back_r,
    plus_s, plus_r, minus_s, minus_r, pair_s, pair_r, own_sum,
    taps, taps_sib, taps_mine, taps_parts, taps_all,
    send, recv, part_send, part_recv, all_send, all_recv, local_sem,
):
    ctx = lax.axis_index("ctx")
    t = lax.axis_index("tp")
    z = ctx // 4
    yh = lax.rem(ctx // 2, 2)
    core = lax.rem(ctx, 2)
    x = t // 2
    yl = lax.rem(t, 2)
    chip = ctx // 2

    def ctx_of(zz, hh, cc):
        return lax.rem(zz + 8, 8) * 4 + hh * 2 + cc

    def tp_of(xx, ll):
        return lax.rem(xx + 4, 4) * 2 + ll

    x_plus = (ctx, tp_of(x + 1, yl))
    x_minus = (ctx, tp_of(x - 1, yl))
    y_low = (ctx, tp_of(x, 1 - yl))
    z_plus = (ctx_of(z + 1, yh, core), t)
    z_minus = (ctx_of(z - 1, yh, core), t)
    y_high = (ctx_of(z, 1 - yh, core), t)
    sibling = (ctx_of(z, yh, 1 - core), t)
    after = (lax.rem(ctx + 1, 32), t)
    before = (lax.rem(ctx + 31, 32), t)
    beyond = (lax.rem(ctx + 31 + 2 * core, 32), t)

    def chip_device(other):
        return (other * 2 + core, t)

    started = []

    def push(src, dst, device):
        slot = len(started)
        copy = pltpu.make_async_remote_copy(
            src_ref=src, dst_ref=dst, send_sem=send.at[slot], recv_sem=recv.at[slot],
            device_id=device, device_id_type=MESH,
        )
        copy.start()
        started.append(copy)
        return copy

    own_copies = [pltpu.make_async_copy(w_hbm, W.at[ctx], local_sem.at[4])]
    for part in range(4):
        own_copies.append(
            pltpu.make_async_copy(
                g_hbm.at[:, lanes(part)], G.at[t, part // 2, part % 2], local_sem.at[part]
            )
        )
    for copy in own_copies:
        copy.start()

    barrier = pltpu.get_barrier_semaphore()
    for device in (x_plus, x_minus, y_low, sibling, beyond):
        pl.semaphore_signal(barrier, inc=1, device_id=device, device_id_type=MESH)

    def greet(step, carry):
        pl.semaphore_signal(
            barrier, inc=1, device_id=chip_device(lax.rem(chip + step, 16)), device_id_type=MESH
        )
        return carry

    lax.fori_loop(1, 16, greet, 0)

    for g in range(4):
        product = (k_ref[:, lanes(g)].astype(F32) * v_ref[:, lanes(g)].astype(F32)).astype(BF16)
        halo_s[:, lanes(g)] = product[384:]
        ext[g, 128:] = product.astype(F32)
        filt[g] = f_ref[:, lanes(g)]
    for copy in own_copies:
        copy.wait()
    pl.semaphore_wait(barrier, 20)

    halo = push(halo_s, halo_r, after)
    w_high = push(W.at[ctx], W.at[ctx], y_high)
    w_plus = {}
    w_minus = {}
    w_plus[1, 0] = push(W.at[ctx], W.at[ctx], z_plus)
    w_minus[1, 0] = push(W.at[ctx], W.at[ctx], z_minus)
    g_plus = push(G.at[t], G.at[t], x_plus)
    g_minus = push(G.at[t], G.at[t], x_minus)
    g_low = push(G.at[t], G.at[t], y_low)
    to_sib = []

    def share_w(slot):
        to_sib.append(push(W.at[slot], W.at[slot], sibling))

    def share_g(j):
        to_sib.append(push(G.at[j, :, 1 - core], S.at[j], sibling))

    share_w(ctx)
    share_g(t)

    def forward_w(step, b):
        hh = yh if b == 0 else 1 - yh
        if step == 0:
            w_high.wait_recv()
            slot = ctx_of(z, 1 - yh, core)
            w_plus[1, 1] = push(W.at[slot], W.at[slot], z_plus)
            w_minus[1, 1] = push(W.at[slot], W.at[slot], z_minus)
            share_w(slot)
            return
        w_plus[step, b].wait_recv()
        w_minus[step, b].wait_recv()
        low = ctx_of(z - step, hh, core)
        high = ctx_of(z + step, hh, core)
        if step < 3:
            w_plus[step + 1, b] = push(W.at[low], W.at[low], z_plus)
            w_minus[step + 1, b] = push(W.at[high], W.at[high], z_minus)
        elif step == 3:
            w_plus[4, b] = push(W.at[low, pl.ds(0, 64)], W.at[low, pl.ds(0, 64)], z_plus)
            w_minus[4, b] = push(W.at[high, pl.ds(64, 64)], W.at[high, pl.ds(64, 64)], z_minus)
        share_w(low)
        if step < 4:
            share_w(high)

    def forward_taps(b):
        def one(g, carry):
            def residue(r, acc):
                window = ext[g, pl.ds(b * 128 + 8 - r, 248), :]
                for k in range(16):
                    acc = acc + filt[g, pl.ds(8 * k + r, 1), :] * window[8 * (15 - k) : 8 * (15 - k) + 128]
                return acc

            conv[g, pl.ds(b * 128, 128), :] = lax.fori_loop(0, 8, residue, jnp.zeros((128, 128), F32))
            return carry

        lax.fori_loop(0, 4, one, 0)

    forward_taps(1)
    forward_w(0, 1)
    forward_w(1, 0)
    forward_taps(2)
    forward_w(1, 1)
    forward_taps(3)
    forward_w(2, 0)
    halo.wait_recv()
    for g in range(4):
        rim = halo_r[:, lanes(g)].astype(F32)
        ext[g, :128] = jnp.where(ctx == 0, 0.0, rim)
    forward_taps(0)
    forward_w(2, 1)

    b_minus, b_plus, b_far = tp_of(x - 1, yl), tp_of(x + 1, yl), tp_of(x + 2, yl)
    p_own, p_minus, p_plus, p_far = (
        tp_of(x, 1 - yl), tp_of(x - 1, 1 - yl), tp_of(x + 1, 1 - yl), tp_of(x + 2, 1 - yl)
    )

    def rows(j, start, size):
        return G.at[j, :, :, pl.ds(start, size)]

    def push_rows(j, start, size, device):
        return push(rows(j, start, size), rows(j, start, size), device)

    g_low.wait_recv()
    a_plus = push_rows(p_own, 112, 288, x_plus)
    a_minus = push_rows(p_own, 112, 288, x_minus)
    g_plus.wait_recv()
    half_plus = push_rows(b_minus, 0, 256, x_plus)
    low_rows = [push_rows(b_minus, 0, 112, y_low), push_rows(b_minus, 400, 112, y_low)]
    g_minus.wait_recv()
    half_minus = push_rows(b_plus, 256, 256, x_minus)
    low_rows += [push_rows(b_plus, 0, 112, y_low), push_rows(b_plus, 400, 112, y_low)]
    share_g(p_own)
    share_g(b_minus)
    share_g(b_plus)
    forward_w(3, 0)

    for g in range(4):
        gated = (q_ref[:, lanes(g)].astype(F32) * conv[g]).astype(BF16)
        gt_own[pl.ds(g * 128, 128), :] = gated.astype(F32).T.astype(BF16)
    gt_copy = push(gt_own, gt_sib, sibling)

    forward_w(3, 1)
    a_plus.wait_recv()
    far_plus = push_rows(p_minus, 112, 144, x_plus)
    a_minus.wait_recv()
    far_minus = push_rows(p_plus, 256, 144, x_minus)
    half_plus.wait_recv()
    low_rows.append(push_rows(b_far, 0, 112, y_low))
    half_minus.wait_recv()
    low_rows.append(push_rows(b_far, 400, 112, y_low))
    share_g(b_far)
    forward_w(4, 0)
    forward_w(4, 1)
    low_rows[0].wait_recv()
    low_rows[1].wait_recv()
    share_g(p_minus)
    low_rows[2].wait_recv()
    low_rows[3].wait_recv()
    share_g(p_plus)
    far_plus.wait_recv()
    far_minus.wait_recv()
    low_rows[4].wait_recv()
    low_rows[5].wait_recv()
    share_g(p_far)
    gt_copy.wait_recv()
    for copy in to_sib:
        copy.wait_recv()

    def term(j, h):
        mine = jnp.concatenate([G[j, yh, core], G[j, 1 - yh, core]], axis=1)
        theirs = jnp.concatenate([S[j, yh], S[j, 1 - yh]], axis=1)
        part = pl.ds(h * 256, 256)
        return jnp.dot(gt_own[part, :], mine, preferred_element_type=F32) + jnp.dot(
            gt_sib[part, :], theirs, preferred_element_type=F32
        )

    sent_plus = {}
    sent_minus = {}

    def send_plus(step, h):
        total = term(lax.rem(z + 5 - step, 8), h)
        if (step - 1, h) in sent_plus:
            sent_plus[step - 1, h].wait_recv()
            total = total + plus_r[step - 2, h].astype(F32)
        plus_s[step - 1, h] = total.astype(BF16)
        sent_plus[step, h] = push(plus_s.at[step - 1, h], plus_r.at[step - 1, h], z_plus)

    def send_minus(step, h):
        total = term(lax.rem(z + 3 + step, 8), h)
        if (step - 1, h) in sent_minus:
            sent_minus[step - 1, h].wait_recv()
            total = total + minus_r[step - 2, h].astype(F32)
        minus_s[step - 1, h] = total.astype(BF16)
        sent_minus[step, h] = push(minus_s.at[step - 1, h], minus_r.at[step - 1, h], z_minus)

    send_plus(1, 0)
    send_minus(1, 1)
    send_plus(2, 1)
    send_minus(2, 0)

    gg[...] = jnp.zeros((512, 512), F32)

    def gather_dot(j, carry):
        block = jnp.concatenate([G[j, 0, 0], G[j, 0, 1], G[j, 1, 0], G[j, 1, 1]], axis=1)
        gg[...] += jnp.dot(
            block, W[pl.ds(4 * j, 4)].reshape(512, 512), preferred_element_type=F32
        )
        return carry

    lax.fori_loop(0, 8, gather_dot, 0)
    for g in range(4):
        grad = gg[:, lanes(g)]
        gq_ref[:, lanes(g)] = (grad * conv[g]).astype(BF16)
        acc = grad * q_ref[:, lanes(g)].astype(F32)
        ga[g, :512] = acc
        back_s[:, lanes(g)] = acc[:128].astype(BF16)
    back = push(back_s, back_r, before)

    def filter_taps(g):
        def residue(r, carry):
            def block(b, sums):
                acc = ga[g, pl.ds(pl.multiple_of(b * 128, 128), 128), :].reshape(16, 8, 128)
                window = ext[g, pl.ds(b * 128 + 8 - r, 248), :].reshape(31, 8, 128)
                return tuple(
                    sums[k] + jnp.sum(acc * window[15 - k : 31 - k], axis=0) for k in range(16)
                )

            sums = lax.fori_loop(0, 4, block, tuple(jnp.zeros((8, 128), F32) for _ in range(16)))
            for k in range(16):
                taps[g, pl.ds(8 * k + r, 1), :] = jnp.sum(sums[k], axis=0, keepdims=True)
            return carry

        lax.fori_loop(0, 8, residue, 0)

    def adjoint_taps(g):
        def block(b, carry):
            here = pl.ds(pl.multiple_of(b * 128, 128), 128)

            def residue(r, acc):
                window = ga[g, pl.ds(b * 128 + r, 248), :]
                for k in range(16):
                    acc = acc + filt[g, pl.ds(8 * k + r, 1), :] * window[8 * k : 8 * k + 128]
                return acc

            grad = lax.fori_loop(0, 8, residue, jnp.zeros((128, 128), F32))
            gk_ref[here, lanes(g)] = (grad * v_ref[here, lanes(g)].astype(F32)).astype(BF16)
            gv_ref[here, lanes(g)] = (grad * k_ref[here, lanes(g)].astype(F32)).astype(BF16)
            return carry

        lax.fori_loop(0, 4, block, 0)

    send_plus(2, 0)
    send_minus(2, 1)
    filter_taps(0)
    send_plus(3, 1)
    send_minus(3, 0)
    filter_taps(1)
    send_plus(3, 0)
    send_minus(3, 1)
    filter_taps(2)
    send_plus(4, 1)
    send_minus(4, 0)
    filter_taps(3)
    half = pl.ds(2 * core, 2)
    other_half = pl.ds(2 - 2 * core, 2)
    tap_pair = push(taps.at[other_half], taps_sib, sibling)
    send_plus(4, 0)
    send_minus(4, 1)

    back.wait_recv()
    for g in range(4):
        rim = back_r[:, lanes(g)].astype(F32)
        ga[g, 512:] = jnp.where(ctx == 31, 0.0, rim)
    adjoint_taps(0)

    tap_pair.wait_recv()
    taps_mine[...] = taps[half] + taps_sib[...]

    def piece(ref, owner):
        return ref.at[:, pl.ds(pl.multiple_of(owner * 8, 8), 8), :]

    def part_copy(step):
        owner = lax.rem(chip + step, 16)
        return pltpu.make_async_remote_copy(
            src_ref=piece(taps_mine, owner), dst_ref=taps_parts.at[step],
            send_sem=part_send.at[step], recv_sem=part_recv.at[step],
            device_id=chip_device(owner), device_id_type=MESH,
        )

    def all_copy(step):
        return pltpu.make_async_remote_copy(
            src_ref=taps_parts.at[0], dst_ref=piece(taps_all.at[half], chip),
            send_sem=all_send.at[step], recv_sem=all_recv.at[step],
            device_id=chip_device(lax.rem(chip + step, 16)), device_id_type=MESH,
        )

    def loop(action):
        def body(step, carry):
            action(step)
            return carry

        lax.fori_loop(1, 16, body, 0)

    loop(lambda step: part_copy(step).start())
    adjoint_taps(1)
    loop(lambda step: part_copy(step).wait_recv())
    mine = pl.ds(pl.multiple_of(chip * 8, 8), 8)
    total = taps_mine[:, mine, :]
    for step in range(1, 16):
        total = total + taps_parts[step]
    taps_parts[0] = total
    taps_all[half, mine, :] = total
    loop(lambda step: all_copy(step).start())

    for h in range(2):
        total = term(z, h)
        sent_plus[4, h].wait_recv()
        sent_minus[4, h].wait_recv()
        total = total + plus_r[3, h].astype(F32) + minus_r[3, h].astype(F32)
        own_sum[pl.ds(h * 256, 256), :] = total[:, :128]
        pair_s[pl.ds(h * 256, 256), :] = total[:, 128:].astype(BF16)
    pair = push(pair_s, pair_r, y_high)
    adjoint_taps(2)
    loop(lambda step: all_copy(step).wait_recv())
    spread = push(taps_all.at[half], taps_all.at[half], sibling)
    adjoint_taps(3)
    pair.wait_recv()
    gw_ref[...] = (own_sum[...] + pair_r[...].astype(F32)).T.astype(BF16)
    spread.wait_recv()
    for g in range(4):
        gf_ref[:, lanes(g)] = taps_all[g]
    for copy in started:
        copy.wait_send()
    loop(lambda step: part_copy(step).wait_send())
    loop(lambda step: all_copy(step).wait_send())


def local(query_act, key_act, value_act, filters, out_weight, grad_out):
    vmem = pl.BlockSpec(memory_space=pltpu.VMEM)
    hbm = pl.BlockSpec(memory_space=pl.ANY)
    shape = jax.ShapeDtypeStruct
    tokens = shape((512, 512), BF16)
    return pl.pallas_call(
        kernel,
        out_shape=(tokens, tokens, tokens, shape((128, 512), F32), shape((128, 512), BF16)),
        in_specs=[vmem, vmem, vmem, vmem, hbm, hbm],
        out_specs=(vmem,) * 5,
        scratch_shapes=[
            pltpu.VMEM((8, 2, 2, 512, 128), BF16),
            pltpu.VMEM((8, 2, 512, 128), BF16),
            pltpu.VMEM((32, 128, 512), BF16),
            pltpu.VMEM((4, 640, 128), F32),
            pltpu.VMEM((4, 512, 128), F32),
            pltpu.VMEM((4, 640, 128), F32),
            pltpu.VMEM((512, 512), F32),
            pltpu.VMEM((4, 128, 128), F32),
            pltpu.VMEM((512, 512), BF16),
            pltpu.VMEM((512, 512), BF16),
            pltpu.VMEM((128, 512), BF16),
            pltpu.VMEM((128, 512), BF16),
            pltpu.VMEM((128, 512), BF16),
            pltpu.VMEM((128, 512), BF16),
            pltpu.VMEM((4, 2, 256, 256), BF16),
            pltpu.VMEM((4, 2, 256, 256), BF16),
            pltpu.VMEM((4, 2, 256, 256), BF16),
            pltpu.VMEM((4, 2, 256, 256), BF16),
            pltpu.VMEM((512, 128), BF16),
            pltpu.VMEM((512, 128), BF16),
            pltpu.VMEM((512, 128), F32),
            pltpu.VMEM((4, 128, 128), F32),
            pltpu.VMEM((2, 128, 128), F32),
            pltpu.VMEM((2, 128, 128), F32),
            pltpu.VMEM((16, 2, 8, 128), F32),
            pltpu.VMEM((4, 128, 128), F32),
            pltpu.SemaphoreType.DMA((80,)),
            pltpu.SemaphoreType.DMA((80,)),
            pltpu.SemaphoreType.DMA((16,)),
            pltpu.SemaphoreType.DMA((16,)),
            pltpu.SemaphoreType.DMA((16,)),
            pltpu.SemaphoreType.DMA((16,)),
            pltpu.SemaphoreType.DMA((5,)),
        ],
        compiler_params=pltpu.CompilerParams(
            collective_id=0, has_side_effects=True, vmem_limit_bytes=52 * 2**20
        ),
        cost_estimate=pl.CostEstimate(flops=2 * 10**9 * 2, bytes_accessed=5 * 2**20, transcendentals=0),
        name="block_grads",
    )(query_act, key_act, value_act, filters, out_weight, grad_out)


def solution(mesh):
    placed = (
        P("ctx", "tp"),
        P("ctx", "tp"),
        P("ctx", "tp"),
        P(None, "tp"),
        P("ctx", "tp"),
        P("ctx", "tp"),
    )
    return jax.shard_map(
        local,
        mesh=mesh,
        in_specs=placed,
        out_specs=(P("ctx", "tp"), P("ctx", "tp"), P("ctx", "tp"), P(None, "tp"), P("ctx", "tp")),
        check_vma=False,
    )
```

time: 671 us -> 102 us (0.15)
  waiting for transfers between devices: 496 us -> 0 us
  Pallas kernels: 0 us -> 94.8 us
  other arithmetic: 94 us -> 0 us
  local copies, waits for them, and re-layouts: 30.5 us -> 6.02 us
  matrix products: 17.3 us -> 0 us
  starting transfers between devices: 13.6 us -> 0 us
  between operations: 13.9 us -> 0.65 us
    psum x1 -> x0, waiting for transfers between devices: 255 us -> none  [local(): grad_filters = lax.psum(filter_grad(grad_acc, extended, taps), 'ctx')]
    all_gather x3 -> x0, waiting for transfers between devices: 189 us -> none  [the longest x1 92.6 us: local(): lax.all_gather(out_weight, 'ctx', axis=0, tiled=True)]
    pallas_call x0 -> x1, Pallas kernels: none -> 94.8 us  [local(): pl.pallas_call(kernel, out_shape=(tokens, tokens, tokens, shape((128, 512...]
    add x16 -> x0, other arithmetic: 57.1 us -> none  [tap_step(): total = total + row * window]
    all_to_all x1 -> x0, waiting for transfers between devices: 49.7 us -> none  [local(): lax.all_to_all(full_grad, 'ctx', split_axis=1, concat_axis=0, tiled=True)]
    reduce_sum x8 -> x0, other arithmetic: 31.8 us -> none  [filter_step(): rows.append(jnp.sum(grad_acc * window, axis=0))]
    dynamic_slice x16 -> x0, local copies, waits for them, and re-layouts: 18.1 us -> none  [tap_step(): row = lax.dynamic_slice_in_dim(filters, tap, 1, 0)]
    dot_general x2 -> x0, matrix products: 17.3 us -> none  [the longest x1 11.5 us: local(): lax.dot_general(owned, lax.all_gather(gated, 'ctx', axis=0, tiled=True),...]
  transfers between devices with their start and end apart: 7 -> 0, of which waited for: 6 -> 0; matrix products, arithmetic and copies ran while one was open for 19% -> 0% of each run, Pallas kernels for 0% -> 0%
where the time goes in v1:
time: 102 us
  Pallas kernels  94.8 us (93%)
  local copies, waits for them, and re-layouts  6.02 us (6%)
    pallas_call x1, Pallas kernels, local(): pl.pallas_call(kernel, out_shape=(tokens, tokens, tokens, shape((128, 512...  94.8 us
    unnamed x11, local copies, waits for them, and re-layouts  6.02 us

profile of v1, /device:TPU:1, one launch (start us, length us, event | category | flops | bytes accessed | tf_op | source)
XLA Modules:
  0.0 101.5 jit_solution(2045984974646546898)
XLA Ops:
  0.6 0.0 copy-start
  0.6 0.9 copy-done
  1.6 0.0 copy-start.1
  1.6 0.9 copy-done.1
  2.5 94.8 %block_grads.1 = (bf16[512,512]{1,0:T(8,128)(2,1)S(1)}, bf16[512,512]{1,0:T(8,128)(2,1)S(1)}, bf16[512,512]{1,0:T(8,128)(2,1)}, f32[128,512]{1,0:T(8,128)S(1)}, bf16[128,512]{1,0:T(8,128)(2,1)S(1)}) custom-call(bf16[512,512]{1,0:T(8,128)(2,1)} %q_ref.1, bf16[512,512]{1,0:T(8,128)(2,1)} %k_ref.1, bf16[512,512]{1,0:T(8,128)(2,1)} %v_ref.1, ...), custom_call_target="tpu_custom_call" | custom-call | flops 4000000000 | bytes 5242880 | tf_op jit(solution)/shard_map/block_grads/pallas_call | solution.py:399
  97.3 0.8 copy.16
  98.1 0.0 copy-start.2
  98.1 0.8 copy.17
  98.9 0.4 copy-done.2
  99.4 0.8 copy.18
  100.1 0.7 copy.19
  100.9 0.7 copy.20
Async XLA Ops:
  0.6 1.0 copy-start
  1.6 0.9 copy-start.1
  98.1 1.2 %copy-start.2 = (bf16[512,512]{1,0:T(8,128)(2,1)S(1)}, bf16[512,512]{1,0:T(8,128)(2,1)}, u32[]{:S(2)}) copy-start(bf16[512,512]{1,0:T(8,128)(2,1)} %get-tuple-element.12) | copy-start | bytes 1572868

commit v2 on v1

v2 whole, which is shorter than its diff:
```python
import jax
import jax.numpy as jnp
from jax import lax
from jax.experimental import pallas as pl
from jax.experimental.pallas import tpu as pltpu
from jax.sharding import PartitionSpec as P

MESH = pl.DeviceIdType.MESH
BF16 = jnp.bfloat16
F32 = jnp.float32


def lanes(group):
    return pl.ds(group * 128, 128)


LEVELS = 2
LEAF = 16 >> LEVELS
SUMS = 3**LEVELS * LEAF


def split_taps(taps, levels):
    if levels == 0:
        return list(taps)
    even, odd = taps[0::2], taps[1::2]
    both = [a + b for a, b in zip(even, odd)]
    return (
        split_taps(both, levels - 1) + split_taps(even, levels - 1) + split_taps(odd, levels - 1)
    )


def split_rows(rows, levels):
    if levels == 0:
        return [rows]
    even, odd = rows[0::2], rows[1::2]
    here = [a - b for a, b in zip(even[:-1], odd)]
    moved = [a - b for a, b in zip(even[1:], odd)]
    return (
        split_rows(odd, levels - 1) + split_rows(here, levels - 1) + split_rows(moved, levels - 1)
    )


def join_sums(sums, levels):
    if levels == 0:
        return list(sums)
    third = len(sums) // 3
    both, even, odd = (
        join_sums(sums[i * third : (i + 1) * third], levels - 1) for i in range(3)
    )
    joined = []
    for p, a, b in zip(both, even, odd):
        joined += [p + a, p + b]
    return joined


def add_taps(sums, window, tap):
    vectors = [window[8 * i : 8 * i + 8] for i in range(31)]
    result = []
    for leaf, rows in enumerate(split_rows(vectors, LEVELS)):
        taps = [tap(leaf * LEAF + k) for k in range(LEAF)]
        for m in range(LEAF):
            total = sums[leaf * LEAF + m]
            for k in range(LEAF):
                total = total + taps[k] * rows[m + k]
            result.append(total)
    return tuple(result)


def no_sums():
    return tuple(jnp.zeros((8, 128), F32) for _ in range(SUMS))


def kernel(
    q_hbm, k_hbm, v_hbm, f_hbm, w_hbm, g_hbm,
    gq_hbm, gk_hbm, gv_hbm, gf_hbm, gw_hbm,
    q_ref, k_ref, v_ref, gq_ref, gk_ref, gv_ref, gw_ref,
    G, S, W, ext, conv, ga, gg, filt, filt_ahead, filt_back, cotangent, gt_own, gt_sib,
    halo_s, halo_r, back_s, back_r,
    part, plus_s, plus_r, minus_s, minus_r, pair_s, pair_r,
    taps, taps_sib, taps_mine, taps_parts, taps_all,
    send, recv, part_send, part_recv, all_send, all_recv, in_sem, out_sem,
):
    ctx = lax.axis_index("ctx")
    t = lax.axis_index("tp")
    z = ctx // 4
    yh = lax.rem(ctx // 2, 2)
    core = lax.rem(ctx, 2)
    x = t // 2
    yl = lax.rem(t, 2)
    chip = ctx // 2

    def ctx_of(zz, hh, cc):
        return lax.rem(zz + 8, 8) * 4 + hh * 2 + cc

    def tp_of(xx, ll):
        return lax.rem(xx + 4, 4) * 2 + ll

    x_plus = (ctx, tp_of(x + 1, yl))
    x_minus = (ctx, tp_of(x - 1, yl))
    y_low = (ctx, tp_of(x, 1 - yl))
    z_plus = (ctx_of(z + 1, yh, core), t)
    z_minus = (ctx_of(z - 1, yh, core), t)
    y_high = (ctx_of(z, 1 - yh, core), t)
    sibling = (ctx_of(z, yh, 1 - core), t)
    after = (lax.rem(ctx + 1, 32), t)
    before = (lax.rem(ctx + 31, 32), t)
    beyond = (lax.rem(ctx + 31 + 2 * core, 32), t)

    def chip_device(other):
        return (other * 2 + core, t)

    started = []

    def push(src, dst, device):
        slot = len(started)
        copy = pltpu.make_async_remote_copy(
            src_ref=src, dst_ref=dst, send_sem=send.at[slot], recv_sem=recv.at[slot],
            device_id=device, device_id_type=MESH,
        )
        copy.start()
        started.append(copy)
        return copy

    barrier = pltpu.get_barrier_semaphore()
    for device in (x_plus, x_minus, y_low, sibling, beyond):
        pl.semaphore_signal(barrier, inc=1, device_id=device, device_id_type=MESH)

    def greet(step, carry):
        pl.semaphore_signal(
            barrier, inc=1, device_id=chip_device(lax.rem(chip + step, 16)), device_id_type=MESH
        )
        return carry

    lax.fori_loop(1, 16, greet, 0)

    loads = []

    def load(src, dst):
        copy = pltpu.make_async_copy(src, dst, in_sem.at[len(loads)])
        copy.start()
        loads.append(copy)

    for g in range(4):
        load(g_hbm.at[:, lanes(g)], G.at[t, g // 2, g % 2])
    load(w_hbm, W.at[ctx])
    load(k_hbm, k_ref)
    load(v_hbm, v_ref)
    for g in range(4):
        load(f_hbm.at[:, lanes(g)], filt.at[g])
    load(q_hbm, q_ref)

    stores = []

    def store(src, dst):
        copy = pltpu.make_async_copy(src, dst, out_sem.at[len(stores)])
        copy.start()
        stores.append(copy)

    for copy in loads[:5]:
        copy.wait()
    pl.semaphore_wait(barrier, 20)

    pieces = ((1 - yh, 256, 256, 48), (yh, 256, 256, 48), (1 - yh, 0, 256, 48), (yh, 0, 256, 48))
    b_minus, b_plus, b_far = tp_of(x - 1, yl), tp_of(x + 1, yl), tp_of(x + 2, yl)
    p_own, p_minus, p_plus, p_far = (
        tp_of(x, 1 - yl), tp_of(x - 1, 1 - yl), tp_of(x + 1, 1 - yl), tp_of(x + 2, 1 - yl)
    )
    flight = {}
    shared = {}

    def push_rows(p, j, start, size, device):
        hs, first = pieces[p][:2]
        ref = G.at[j, hs, :, pl.ds(first + start, size)]
        return push(ref, ref, device)

    def share_g(p, j):
        hs, first, count, edge = pieces[p]
        here = pl.ds(first, count)
        shared.setdefault(p, []).append(
            push(G.at[j, hs, 1 - core, here], S.at[j, hs, here], sibling)
        )

    def gather_0(p):
        count = pieces[p][2]
        flight[p, "plus"] = push_rows(p, t, 0, count, x_plus)
        flight[p, "minus"] = push_rows(p, t, 0, count, x_minus)
        flight[p, "low"] = push_rows(p, t, 0, count, y_low)
        share_g(p, t)

    def gather_1(p):
        hs, first, count, edge = pieces[p]
        half = count // 2
        flight[p, "low"].wait_recv()
        flight[p, "a_plus"] = push_rows(p, p_own, edge, count - 2 * edge, x_plus)
        flight[p, "a_minus"] = push_rows(p, p_own, edge, count - 2 * edge, x_minus)
        flight[p, "plus"].wait_recv()
        flight[p, "half_plus"] = push_rows(p, b_minus, 0, half, x_plus)
        flight[p, "low_0"] = push_rows(p, b_minus, 0, edge, y_low)
        flight[p, "low_1"] = push_rows(p, b_minus, count - edge, edge, y_low)
        flight[p, "minus"].wait_recv()
        flight[p, "half_minus"] = push_rows(p, b_plus, half, half, x_minus)
        flight[p, "low_2"] = push_rows(p, b_plus, 0, edge, y_low)
        flight[p, "low_3"] = push_rows(p, b_plus, count - edge, edge, y_low)
        share_g(p, p_own)
        share_g(p, b_minus)
        share_g(p, b_plus)

    def gather_2(p):
        hs, first, count, edge = pieces[p]
        half = count // 2
        flight[p, "a_plus"].wait_recv()
        flight[p, "far_plus"] = push_rows(p, p_minus, edge, half - edge, x_plus)
        flight[p, "a_minus"].wait_recv()
        flight[p, "far_minus"] = push_rows(p, p_plus, half, half - edge, x_minus)
        flight[p, "half_plus"].wait_recv()
        flight[p, "low_4"] = push_rows(p, b_far, 0, edge, y_low)
        flight[p, "half_minus"].wait_recv()
        flight[p, "low_5"] = push_rows(p, b_far, count - edge, edge, y_low)
        share_g(p, b_far)

    def gather_3(p):
        for name in ("low_0", "low_1"):
            flight[p, name].wait_recv()
        share_g(p, p_minus)
        for name in ("low_2", "low_3"):
            flight[p, name].wait_recv()
        share_g(p, p_plus)
        for name in ("far_plus", "far_minus", "low_4", "low_5"):
            flight[p, name].wait_recv()
        share_g(p, p_far)

    w_plus = {}
    w_minus = {}
    w_shared = []

    def share_w(slot):
        w_shared.append(push(W.at[slot], W.at[slot], sibling))

    def forward_w(step, b):
        hh = yh if b == 0 else 1 - yh
        if step == 0:
            w_high.wait_recv()
            slot = ctx_of(z, 1 - yh, core)
            w_plus[1, 1] = push(W.at[slot], W.at[slot], z_plus)
            w_minus[1, 1] = push(W.at[slot], W.at[slot], z_minus)
            share_w(slot)
            return
        w_plus[step, b].wait_recv()
        w_minus[step, b].wait_recv()
        low = ctx_of(z - step, hh, core)
        high = ctx_of(z + step, hh, core)
        if step < 3:
            w_plus[step + 1, b] = push(W.at[low], W.at[low], z_plus)
            w_minus[step + 1, b] = push(W.at[high], W.at[high], z_minus)
        elif step == 3:
            w_plus[4, b] = push(W.at[low, pl.ds(0, 64)], W.at[low, pl.ds(0, 64)], z_plus)
            w_minus[4, b] = push(W.at[high, pl.ds(64, 64)], W.at[high, pl.ds(64, 64)], z_minus)
        share_w(low)
        if step < 4:
            share_w(high)

    def split_filters():
        for g in range(4):
            by_8 = [filt[g, 8 * k : 8 * k + 8, :] for k in range(16)]
            for i, row in enumerate(split_taps(by_8[::-1], LEVELS)):
                filt_back[g, 8 * i : 8 * i + 8, :] = row
            for i, row in enumerate(split_taps(by_8, LEVELS)):
                filt_ahead[g, 8 * i : 8 * i + 8, :] = row

    def forward_taps(b, group, count):
        def one(g, carry):
            def residue(r, sums):
                return add_taps(
                    sums, ext[g, pl.ds(b * 128 + 8 - r, 248), :],
                    lambda i: jnp.broadcast_to(filt_back[g, pl.ds(8 * i + r, 1), :], (8, 128)),
                )

            for m, row in enumerate(join_sums(lax.fori_loop(0, 8, residue, no_sums()), LEVELS)):
                conv[g, pl.ds(b * 128 + 8 * m, 8), :] = row
            return carry

        lax.fori_loop(group, group + count, one, 0)

    def filter_taps(g, first_block):
        for n in range(2):
            start = (first_block + n) * 128
            by_8 = [ga[g, start + 8 * k : start + 8 * k + 8, :] for k in range(16)]
            for i, row in enumerate(split_taps(by_8, LEVELS)):
                cotangent[n, 8 * i : 8 * i + 8, :] = row

        def residue(r, carry):
            def block(n, sums):
                return add_taps(
                    sums, ext[g, pl.ds((first_block + n) * 128 + 8 - r, 248), :],
                    lambda i: cotangent[n, 8 * i : 8 * i + 8, :],
                )

            sums = join_sums(lax.fori_loop(0, 2, block, no_sums()), LEVELS)
            for k in range(16):
                row = jnp.sum(sums[15 - k], axis=0, keepdims=True)
                if first_block == 0:
                    row += taps[g, pl.ds(8 * k + r, 1), :]
                taps[g, pl.ds(8 * k + r, 1), :] = row
            return carry

        lax.fori_loop(0, 8, residue, 0)

    def adjoint_taps(b):
        def one(g, carry):
            def residue(r, sums):
                return add_taps(
                    sums, ga[g, pl.ds(b * 128 + r, 248), :],
                    lambda i: jnp.broadcast_to(filt_ahead[g, pl.ds(8 * i + r, 1), :], (8, 128)),
                )

            sums = join_sums(lax.fori_loop(0, 8, residue, no_sums()), LEVELS)
            side = pl.ds(pl.multiple_of(g * 128, 128), 128)
            for m in range(0, 16, 2):
                here = pl.ds(b * 128 + 8 * m, 16)
                grad = jnp.concatenate([sums[m], sums[m + 1]], axis=0)
                gk_ref[here, side] = (grad * v_ref[here, side].astype(F32)).astype(BF16)
                gv_ref[here, side] = (grad * k_ref[here, side].astype(F32)).astype(BF16)
            return carry

        lax.fori_loop(0, 4, one, 0)

    def terms(r, s):
        hs = 1 - yh if r == 0 else yh
        ahead = lax.rem(z + 4 - s, 8)
        behind = lax.rem(z + 4 + s, 8) if s else z
        mine = jnp.concatenate([G[ahead, hs, core], G[behind, hs, core]], axis=1)
        theirs = jnp.concatenate([S[ahead, hs], S[behind, hs]], axis=1)
        part[r, s] = jnp.dot(gt_own[...], mine, preferred_element_type=F32) + jnp.dot(
            gt_sib[...], theirs, preferred_element_type=F32
        )

    sent_plus = {}
    sent_minus = {}

    def send_plus(r, step, h):
        total = part[r, step - 1, pl.ds(256 * h, 256), :128]
        if (r, step - 1, h) in sent_plus:
            sent_plus[r, step - 1, h].wait_recv()
            total = total + plus_r[r, step - 2, h].astype(F32)
        plus_s[r, step - 1, h] = total.astype(BF16)
        sent_plus[r, step, h] = push(plus_s.at[r, step - 1, h], plus_r.at[r, step - 1, h], z_plus)

    def send_minus(r, step, h):
        columns = pl.ds(0 if step == 1 else 128, 128)
        total = part[r, step - 1, pl.ds(256 * h, 256), columns]
        if (r, step - 1, h) in sent_minus:
            sent_minus[r, step - 1, h].wait_recv()
            total = total + minus_r[r, step - 2, h].astype(F32)
        minus_s[r, step - 1, h] = total.astype(BF16)
        sent_minus[r, step, h] = push(
            minus_s.at[r, step - 1, h], minus_r.at[r, step - 1, h], z_minus
        )

    def reduce_start(r):
        terms(r, 0)
        send_plus(r, 1, 0)
        send_minus(r, 1, 1)
        terms(r, 1)
        send_plus(r, 2, 1)
        send_minus(r, 2, 0)
        terms(r, 2)
        terms(r, 3)

    def reduce_step(r, n):
        step, late = ((2, 1), (3, 0), (3, 1), (4, 0), (4, 1))[n]
        send_plus(r, step, 1 - late)
        send_minus(r, step, late)

    def reduced(r, h):
        sent_plus[r, 4, h].wait_recv()
        sent_minus[r, 4, h].wait_recv()
        return (
            part[r, 0, pl.ds(256 * h, 256), 128:]
            + plus_r[r, 3, h].astype(F32)
            + minus_r[r, 3, h].astype(F32)
        )

    def accumulate(first, count):
        here = pl.ds(first, count)
        for n in range(4):
            block = jnp.concatenate(
                [G[2 * n + i // 4, (i // 2) % 2, i % 2, here] for i in range(8)], axis=1
            )
            grad = jnp.dot(block, W[pl.ds(8 * n, 8)].reshape(1024, 512), preferred_element_type=F32)
            gg[here, :] = grad if n == 0 else gg[here, :] + grad

    def finish_rows(first, count):
        here = pl.ds(first, count)
        for g in range(4):
            grad = gg[here, lanes(g)]
            gq_ref[here, lanes(g)] = (grad * conv[g, here, :]).astype(BF16)
            ga[g, here, :] = grad * q_ref[here, lanes(g)].astype(F32)

    def gate(groups):
        for g in groups:
            gated = (q_ref[:, lanes(g)].astype(F32) * conv[g]).astype(BF16)
            gt_own[pl.ds(g * 128, 128), :] = gated.astype(F32).T.astype(BF16)

    half = pl.ds(2 * core, 2)
    other_half = pl.ds(2 - 2 * core, 2)

    def piece(ref, owner):
        return ref.at[:, pl.ds(pl.multiple_of(owner * 8, 8), 8), :]

    def part_copy(step):
        owner = lax.rem(chip + step, 16)
        return pltpu.make_async_remote_copy(
            src_ref=piece(taps_mine, owner), dst_ref=taps_parts.at[step],
            send_sem=part_send.at[step], recv_sem=part_recv.at[step],
            device_id=chip_device(owner), device_id_type=MESH,
        )

    def all_copy(step):
        return pltpu.make_async_remote_copy(
            src_ref=taps_parts.at[0], dst_ref=piece(taps_all.at[half], chip),
            send_sem=all_send.at[step], recv_sem=all_recv.at[step],
            device_id=chip_device(lax.rem(chip + step, 16)), device_id_type=MESH,
        )

    def loop(action):
        def body(step, carry):
            action(step)
            return carry

        lax.fori_loop(1, 16, body, 0)

    gather_0(0)
    w_high = push(W.at[ctx], W.at[ctx], y_high)
    w_plus[1, 0] = push(W.at[ctx], W.at[ctx], z_plus)
    w_minus[1, 0] = push(W.at[ctx], W.at[ctx], z_minus)
    share_w(ctx)
    for copy in loads[5:]:
        copy.wait()
    split_filters()
    for g in range(4):
        product = (k_ref[:, lanes(g)].astype(F32) * v_ref[:, lanes(g)].astype(F32)).astype(BF16)
        halo_s[:, lanes(g)] = product[384:]
        ext[g, 128:] = product.astype(F32)
    halo = push(halo_s, halo_r, after)
    gather_0(1)
    forward_taps(1, 0, 4)
    forward_w(0, 1)
    gather_1(0)
    gather_0(2)
    forward_w(1, 0)
    forward_taps(2, 0, 4)
    gather_1(1)
    forward_taps(3, 0, 3)
    forward_w(1, 1)
    gather_2(0)
    gather_0(3)
    forward_taps(3, 3, 1)
    forward_w(2, 0)
    halo.wait_recv()
    for g in range(4):
        rim = halo_r[:, lanes(g)].astype(F32)
        ext[g, :128] = jnp.where(ctx == 0, 0.0, rim)
    gather_1(2)
    forward_taps(0, 0, 4)
    forward_w(2, 1)
    gate((0,))
    gather_2(1)
    gate((1,))
    forward_w(3, 0)
    gate((2,))
    gather_1(3)
    gate((3,))
    gt_copy = push(gt_own, gt_sib, sibling)
    gather_3(0)
    forward_w(3, 1)
    forward_w(4, 0)
    gather_2(2)
    forward_w(4, 1)
    gather_3(1)
    for copy in w_shared:
        copy.wait_recv()
    accumulate(256, 256)
    finish_rows(256, 256)
    gather_2(3)
    filter_taps(0, 2)
    filter_taps(1, 2)
    gather_3(2)
    gt_copy.wait_recv()
    for p in (0, 2):
        for copy in shared[p]:
            copy.wait_recv()
    reduce_start(0)
    filter_taps(2, 2)
    gather_3(3)
    for p in (1, 3):
        for copy in shared[p]:
            copy.wait_recv()
    reduce_start(1)
    accumulate(0, 256)
    finish_rows(0, 256)
    store(gq_ref, gq_hbm)
    for g in range(4):
        back_s[:, lanes(g)] = ga[g, :128, :].astype(BF16)
    back = push(back_s, back_r, before)
    reduce_step(0, 0)
    filter_taps(3, 2)
    filter_taps(0, 0)
    reduce_step(1, 0)
    filter_taps(1, 0)
    reduce_step(0, 1)
    filter_taps(2, 0)
    reduce_step(1, 1)
    filter_taps(3, 0)
    tap_pair = push(taps.at[other_half], taps_sib, sibling)
    reduce_step(0, 2)
    adjoint_taps(2)
    tap_pair.wait_recv()
    taps_mine[...] = taps[half] + taps_sib[...]
    loop(lambda step: part_copy(step).start())
    reduce_step(1, 2)
    adjoint_taps(1)
    reduce_step(0, 3)
    loop(lambda step: part_copy(step).wait_recv())
    mine = pl.ds(pl.multiple_of(chip * 8, 8), 8)
    total = taps_mine[:, mine, :]
    for step in range(1, 16):
        total = total + taps_parts[step]
    taps_parts[0] = total
    taps_all[half, mine, :] = total
    loop(lambda step: all_copy(step).start())
    reduce_step(1, 3)
    adjoint_taps(0)
    reduce_step(0, 4)
    reduce_step(1, 4)
    back.wait_recv()
    for g in range(4):
        rim = back_r[:, lanes(g)].astype(F32)
        ga[g, 512:] = jnp.where(ctx == 31, 0.0, rim)
    loop(lambda step: all_copy(step).wait_recv())
    spread = push(taps_all.at[half], taps_all.at[half], sibling)
    for h in range(2):
        pair_s[pl.ds(256 * h, 256), :] = reduced(0, h).astype(BF16)
    pair = push(pair_s, pair_r, y_high)
    adjoint_taps(3)
    store(gk_ref, gk_hbm)
    store(gv_ref, gv_hbm)
    spread.wait_recv()
    for g in range(4):
        store(taps_all.at[g], gf_hbm.at[:, lanes(g)])
    totals = [reduced(1, h) for h in range(2)]
    pair.wait_recv()
    for h in range(2):
        rows = pl.ds(256 * h, 256)
        gw_ref[:, rows] = (totals[h] + pair_r[rows, :].astype(F32)).T.astype(BF16)
    store(gw_ref, gw_hbm)
    for copy in started:
        copy.wait_send()
    loop(lambda step: part_copy(step).wait_send())
    loop(lambda step: all_copy(step).wait_send())
    for copy in stores:
        copy.wait()


def local(query_act, key_act, value_act, filters, out_weight, grad_out):
    hbm = pl.BlockSpec(memory_space=pl.ANY)
    shape = jax.ShapeDtypeStruct
    tokens = shape((512, 512), BF16)
    block = pltpu.VMEM((512, 512), BF16)
    rim = pltpu.VMEM((128, 512), BF16)
    sums = pltpu.VMEM((2, 4, 2, 256, 128), BF16)
    return pl.pallas_call(
        kernel,
        out_shape=(tokens, tokens, tokens, shape((128, 512), F32), shape((128, 512), BF16)),
        in_specs=[hbm] * 6,
        out_specs=(hbm,) * 5,
        scratch_shapes=[
            block, block, block, block, block, block, rim,
            pltpu.VMEM((8, 2, 2, 512, 128), BF16),
            pltpu.VMEM((8, 2, 512, 128), BF16),
            pltpu.VMEM((32, 128, 512), BF16),
            pltpu.VMEM((4, 640, 128), F32),
            pltpu.VMEM((4, 512, 128), F32),
            pltpu.VMEM((4, 640, 128), F32),
            pltpu.VMEM((512, 512), F32),
            pltpu.VMEM((4, 128, 128), F32),
            pltpu.VMEM((4, 8 * SUMS, 128), F32),
            pltpu.VMEM((4, 8 * SUMS, 128), F32),
            pltpu.VMEM((2, 8 * SUMS, 128), F32),
            block, block,
            rim, rim, rim, rim,
            pltpu.VMEM((2, 4, 512, 256), F32),
            sums, sums, sums, sums,
            pltpu.VMEM((512, 128), BF16),
            pltpu.VMEM((512, 128), BF16),
            pltpu.VMEM((4, 128, 128), F32),
            pltpu.VMEM((2, 128, 128), F32),
            pltpu.VMEM((2, 128, 128), F32),
            pltpu.VMEM((16, 2, 8, 128), F32),
            pltpu.VMEM((4, 128, 128), F32),
            pltpu.SemaphoreType.DMA((170,)),
            pltpu.SemaphoreType.DMA((170,)),
            pltpu.SemaphoreType.DMA((16,)),
            pltpu.SemaphoreType.DMA((16,)),
            pltpu.SemaphoreType.DMA((16,)),
            pltpu.SemaphoreType.DMA((16,)),
            pltpu.SemaphoreType.DMA((12,)),
            pltpu.SemaphoreType.DMA((8,)),
        ],
        compiler_params=pltpu.CompilerParams(
            collective_id=0, has_side_effects=True, vmem_limit_bytes=60 * 2**20
        ),
        cost_estimate=pl.CostEstimate(flops=4 * 10**9, bytes_accessed=5 * 2**20, transcendentals=0),
        name="block_grads",
    )(query_act, key_act, value_act, filters, out_weight, grad_out)


def solution(mesh):
    placed = (
        P("ctx", "tp"),
        P("ctx", "tp"),
        P("ctx", "tp"),
        P(None, "tp"),
        P("ctx", "tp"),
        P("ctx", "tp"),
    )
    return jax.shard_map(
        local,
        mesh=mesh,
        in_specs=placed,
        out_specs=(P("ctx", "tp"), P("ctx", "tp"), P("ctx", "tp"), P(None, "tp"), P("ctx", "tp")),
        check_vma=False,
    )
```

time: 102 us -> 94 us (0.922)
  Pallas kernels: 94.8 us -> 87.2 us
    pallas_call x1, Pallas kernels: 94.8 us -> 87.2 us  [local(): pl.pallas_call(kernel, out_shape=(tokens, tokens, tokens, shape((128, 512...]
    unnamed x11 -> x13, local copies, waits for them, and re-layouts: 6.02 us -> 5.9 us
where the time goes in v2:
time: 94 us; the launch traced here: 93.8 us
  Pallas kernels  87.2 us (93%)
  local copies, waits for them, and re-layouts  5.9 us (6%)
    pallas_call x1, Pallas kernels, local(): pl.pallas_call(kernel, out_shape=(tokens, tokens, tokens, shape((128, 512...  87.2 us
    unnamed x13, local copies, waits for them, and re-layouts  5.9 us

profile of v2, /device:TPU:1, one launch (start us, length us, event | category | flops | bytes accessed | tf_op | source)
XLA Modules:
  0.0 93.8 jit_solution(15684234139740056410)
XLA Ops:
  0.6 87.2 %block_grads.1 = (bf16[512,512]{1,0:T(8,128)(2,1)}, bf16[512,512]{1,0:T(8,128)(2,1)}, bf16[512,512]{1,0:T(8,128)(2,1)}, f32[128,512]{1,0:T(8,128)}, bf16[128,512]{1,0:T(8,128)(2,1)}) custom-call(bf16[512,512]{1,0:T(8,128)(2,1)} %q_hbm.1, bf16[512,512]{1,0:T(8,128)(2,1)} %k_hbm.1, bf16[512,512]{1,0:T(8,128)(2,1)} %v_hbm.1, f32[128,512]{1,0:T(8,128)} %f_hbm.1, ...), custom_call_target="tpu_custom_call" | custom-call | flops 4000000000 | bytes 5242880 | tf_op jit(solution)/shard_map/block_grads/pallas_call | solution.py:571
  87.9 0.0 copy-start.1
  87.9 1.9 %copy.16 = bf16[512,512]{1,0:T(8,128)(2,1)} copy(bf16[512,512]{1,0:T(8,128)(2,1)} %get-tuple-element.10) | data formatting | bytes 1048576
  89.8 0.0 copy-done.1
  89.8 0.0 copy-start
  89.8 0.8 copy.17
  90.6 0.4 copy-done
  91.0 0.0 copy-start.2
  91.0 0.8 copy.18
  91.8 0.3 copy-done.2
  92.1 0.0 copy-start.3
  92.1 0.7 copy.19
  92.8 0.3 copy-done.3
  93.1 0.7 copy.20
Async XLA Ops:
  87.9 1.9 %copy-start.1 = (bf16[512,512]{1,0:T(8,128)(2,1)S(1)}, bf16[512,512]{1,0:T(8,128)(2,1)}, u32[]{:S(2)}) copy-start(bf16[512,512]{1,0:T(8,128)(2,1)} %get-tuple-element.11) | copy-start | bytes 1572868
  89.8 1.2 %copy-start = (bf16[512,512]{1,0:T(8,128)(2,1)S(1)}, bf16[512,512]{1,0:T(8,128)(2,1)}, u32[]{:S(2)}) copy-start(bf16[512,512]{1,0:T(8,128)(2,1)} %get-tuple-element.12) | copy-start | bytes 1572868
  91.0 1.1 %copy-start.2 = (f32[128,512]{1,0:T(8,128)S(1)}, f32[128,512]{1,0:T(8,128)}, u32[]{:S(2)}) copy-start(f32[128,512]{1,0:T(8,128)} %get-tuple-element.13) | copy-start | bytes 786436
  92.1 1.0 %copy-start.3 = (bf16[128,512]{1,0:T(8,128)(2,1)S(1)}, bf16[128,512]{1,0:T(8,128)(2,1)}, u32[]{:S(2)}) copy-start(bf16[128,512]{1,0:T(8,128)(2,1)} %get-tuple-element.14) | copy-start | bytes 393220

commit v3 on v2

--- a/solution.py
+++ b/solution.py
@@ -122,16 +122,8 @@
         return copy
 
     barrier = pltpu.get_barrier_semaphore()
-    for device in (x_plus, x_minus, y_low, sibling, beyond):
+    for device in (x_plus, x_minus, y_low, z_plus, z_minus, y_high, sibling, beyond):
         pl.semaphore_signal(barrier, inc=1, device_id=device, device_id_type=MESH)
-
-    def greet(step, carry):
-        pl.semaphore_signal(
-            barrier, inc=1, device_id=chip_device(lax.rem(chip + step, 16)), device_id_type=MESH
-        )
-        return carry
-
-    lax.fori_loop(1, 16, greet, 0)
 
     loads = []
 
@@ -158,7 +150,7 @@
 
     for copy in loads[:5]:
         copy.wait()
-    pl.semaphore_wait(barrier, 20)
+    pl.semaphore_wait(barrier, 8)
 
     pieces = ((1 - yh, 256, 256, 48), (yh, 256, 256, 48), (1 - yh, 0, 256, 48), (yh, 0, 256, 48))
     b_minus, b_plus, b_far = tp_of(x - 1, yl), tp_of(x + 1, yl), tp_of(x + 2, yl)
@@ -428,6 +420,15 @@
             return carry
 
         lax.fori_loop(1, 16, body, 0)
+
+    def greet_far():
+        for away in range(8):
+            for hh in range(2):
+                if (away, hh) not in ((0, 0), (1, 0), (7, 0), (0, 1)):
+                    far = ctx_of(lax.rem(z + away, 8), lax.rem(yh + hh, 2), core)
+                    pl.semaphore_signal(
+                        barrier, inc=1, device_id=(far, t), device_id_type=MESH
+                    )
 
     gather_0(0)
     w_high = push(W.at[ctx], W.at[ctx], y_high)
@@ -480,6 +481,7 @@
     for copy in w_shared:
         copy.wait_recv()
     accumulate(256, 256)
+    greet_far()
     finish_rows(256, 256)
     gather_2(3)
     filter_taps(0, 2)
@@ -516,6 +518,7 @@
     adjoint_taps(2)
     tap_pair.wait_recv()
     taps_mine[...] = taps[half] + taps_sib[...]
+    pl.semaphore_wait(barrier, 12)
     loop(lambda step: part_copy(step).start())
     reduce_step(1, 2)
     adjoint_taps(1)
@@ -561,6 +564,15 @@
         copy.wait()
 
 
+def hand_on(*refs):
+    sems = refs[10]
+    copies = [pltpu.make_async_copy(refs[i], refs[5 + i], sems.at[i]) for i in range(5)]
+    for copy in copies:
+        copy.start()
+    for copy in copies:
+        copy.wait()
+
+
 def local(query_act, key_act, value_act, filters, out_weight, grad_out):
     hbm = pl.BlockSpec(memory_space=pl.ANY)
     shape = jax.ShapeDtypeStruct
@@ -568,7 +580,7 @@
     block = pltpu.VMEM((512, 512), BF16)
     rim = pltpu.VMEM((128, 512), BF16)
     sums = pltpu.VMEM((2, 4, 2, 256, 128), BF16)
-    return pl.pallas_call(
+    results = pl.pallas_call(
         kernel,
         out_shape=(tokens, tokens, tokens, shape((128, 512), F32), shape((128, 512), BF16)),
         in_specs=[hbm] * 6,
@@ -612,6 +624,14 @@
         cost_estimate=pl.CostEstimate(flops=4 * 10**9, bytes_accessed=5 * 2**20, transcendentals=0),
         name="block_grads",
     )(query_act, key_act, value_act, filters, out_weight, grad_out)
+    return pl.pallas_call(
+        hand_on,
+        out_shape=(tokens, tokens, tokens, shape((128, 512), F32), shape((128, 512), BF16)),
+        in_specs=[pl.BlockSpec(memory_space=pltpu.VMEM)] * 5,
+        out_specs=(hbm,) * 5,
+        scratch_shapes=[pltpu.SemaphoreType.DMA((5,))],
+        name="hand_on",
+    )(*results)
 
 
 def solution(mesh):

time: 94 us -> 88.8 us (0.945)
  local copies, waits for them, and re-layouts: 5.9 us -> 0 us
    unnamed x13 -> x0, local copies, waits for them, and re-layouts: 5.9 us -> none
    pallas_call x0 -> x1, Pallas kernels: none -> 2.76 us  [local(): pl.pallas_call(hand_on, out_shape=(tokens, tokens, tokens, shape((128, 51...]
    pallas_call x1, Pallas kernels: 87.2 us -> 85.3 us  [local(): pl.pallas_call(kernel, out_shape=(tokens, tokens, tokens, shape((128, 512...]
where the time goes in v3:
time: 88.8 us; the launch traced here: 88.7 us
  Pallas kernels  88.1 us (99%)
    pallas_call x1, Pallas kernels, local(): pl.pallas_call(kernel, out_shape=(tokens, tokens, tokens, shape((128, 512...  85.3 us
    pallas_call x1, Pallas kernels, local(): pl.pallas_call(hand_on, out_shape=(tokens, tokens, tokens, shape((128, 51...  2.76 us

profile of v3, /device:TPU:1, one launch (start us, length us, event | category | flops | bytes accessed | tf_op | source)
XLA Modules:
  0.0 88.7 jit_solution(981974066739667156)
XLA Ops:
  0.6 85.3 %block_grads.1 = (bf16[512,512]{1,0:T(8,128)(2,1)}, bf16[512,512]{1,0:T(8,128)(2,1)}, bf16[512,512]{1,0:T(8,128)(2,1)}, f32[128,512]{1,0:T(8,128)}, bf16[128,512]{1,0:T(8,128)(2,1)}) custom-call(bf16[512,512]{1,0:T(8,128)(2,1)} %q_hbm.1, bf16[512,512]{1,0:T(8,128)(2,1)} %k_hbm.1, bf16[512,512]{1,0:T(8,128)(2,1)} %v_hbm.1, f32[128,512]{1,0:T(8,128)} %f_hbm.1, ...), custom_call_target="tpu_custom_call" | custom-call | flops 4000000000 | bytes 5242880 | tf_op jit(solution)/shard_map/block_grads/pallas_call | solution.py:583
  85.9 2.8 %hand_on.1 = (bf16[512,512]{1,0:T(8,128)(2,1)}, bf16[512,512]{1,0:T(8,128)(2,1)}, bf16[512,512]{1,0:T(8,128)(2,1)}, f32[128,512]{1,0:T(8,128)}, bf16[128,512]{1,0:T(8,128)(2,1)}) custom-call(bf16[512,512]{1,0:T(8,128)(2,1)} %get-tuple-element.10.refs_0_, bf16[512,512]{1,0:T(8,128)(2,1)} %get-tuple-element.11.refs_1_, ...), custom_call_target="tpu_custom_call" | custom-call | tf_op jit(solution)/shard_map/hand_on/pallas_call | solution.py:627

commit v4 on v3

--- a/solution.py
+++ b/solution.py
@@ -565,11 +565,15 @@
 
 
 def hand_on(*refs):
-    sems = refs[10]
-    copies = [pltpu.make_async_copy(refs[i], refs[5 + i], sems.at[i]) for i in range(5)]
-    for copy in copies:
+    held, arrived, left = refs[10:15], refs[15], refs[16]
+    loads = [pltpu.make_async_copy(refs[i], held[i], arrived.at[i]) for i in range(5)]
+    stores = [pltpu.make_async_copy(held[i], refs[5 + i], left.at[i]) for i in range(5)]
+    for copy in loads:
         copy.start()
-    for copy in copies:
+    for i in range(5):
+        loads[i].wait()
+        stores[i].start()
+    for copy in stores:
         copy.wait()
 
 
@@ -627,9 +631,15 @@
     return pl.pallas_call(
         hand_on,
         out_shape=(tokens, tokens, tokens, shape((128, 512), F32), shape((128, 512), BF16)),
-        in_specs=[pl.BlockSpec(memory_space=pltpu.VMEM)] * 5,
+        in_specs=[hbm] * 5,
         out_specs=(hbm,) * 5,
-        scratch_shapes=[pltpu.SemaphoreType.DMA((5,))],
+        scratch_shapes=[
+            block, block, block,
+            pltpu.VMEM((128, 512), F32),
+            rim,
+            pltpu.SemaphoreType.DMA((5,)),
+            pltpu.SemaphoreType.DMA((5,)),
+        ],
         name="hand_on",
     )(*results)
 

time: 88.8 us -> 88.5 us (level)
  no operation moved by 1% of the time
where the time goes in v4:
time: 88.5 us; the launch traced here: 88.3 us
  Pallas kernels  87.7 us (99%)
    pallas_call x1, Pallas kernels, local(): pl.pallas_call(kernel, out_shape=(tokens, tokens, tokens, shape((128, 512...  85.3 us
    pallas_call x1, Pallas kernels, local(): pl.pallas_call(hand_on, out_shape=(tokens, tokens, tokens, shape((128, 51...  2.39 us

profile of v4, /device:TPU:1, one launch (start us, length us, event | category | flops | bytes accessed | tf_op | source)
XLA Modules:
  0.0 88.3 jit_solution(4929154546991649229)
XLA Ops:
  0.6 85.3 %block_grads.1 = (bf16[512,512]{1,0:T(8,128)(2,1)}, bf16[512,512]{1,0:T(8,128)(2,1)}, bf16[512,512]{1,0:T(8,128)(2,1)}, f32[128,512]{1,0:T(8,128)}, bf16[128,512]{1,0:T(8,128)(2,1)}) custom-call(bf16[512,512]{1,0:T(8,128)(2,1)} %q_hbm.1, bf16[512,512]{1,0:T(8,128)(2,1)} %k_hbm.1, bf16[512,512]{1,0:T(8,128)(2,1)} %v_hbm.1, f32[128,512]{1,0:T(8,128)} %f_hbm.1, ...), custom_call_target="tpu_custom_call" | custom-call | flops 4000000000 | bytes 5242880 | tf_op jit(solution)/shard_map/block_grads/pallas_call | solution.py:587
  85.9 2.4 %hand_on.1 = (bf16[512,512]{1,0:T(8,128)(2,1)}, bf16[512,512]{1,0:T(8,128)(2,1)}, bf16[512,512]{1,0:T(8,128)(2,1)}, f32[128,512]{1,0:T(8,128)}, bf16[128,512]{1,0:T(8,128)(2,1)}) custom-call(bf16[512,512]{1,0:T(8,128)(2,1)} %get-tuple-element.10.refs_0_, bf16[512,512]{1,0:T(8,128)(2,1)} %get-tuple-element.11.refs_1_, ...), custom_call_target="tpu_custom_call" | custom-call | tf_op jit(solution)/shard_map/hand_on/pallas_call | solution.py:631
